TPU v7x, 128 devices: a whole 4x4x4 slice. The times are simulated.
128 devices in a mesh: dp: 16 (over z_lo, x, core), ctx: 8 (over z_hi, y).
Axes of the slice: x: 4, y: 4, z: 4 (z_hi: 2, z_lo: 2; z = z_hi * 2 + z_lo), core: 2. Of those that a mesh axis runs over, the one named last changes fastest.
Arguments:
- query_rows: bfloat16 [262144, 128], P(('dp', 'ctx')), may hold values from -256 to 256
- key_rows: bfloat16 [262144, 128], P(('dp', 'ctx')), may hold values from -64 to 64
- value_rows: bfloat16 [262144, 128], P(('dp', 'ctx')), may hold values from -6 to 6
- doc_lens: int32 [16, 4], P('dp'), may hold values from 1 to 12288, 16384 in all within a row
- dest_group: int32 [1024], P(('dp', 'ctx')), may hold values from 0 to 15, as said below
- block_pos: int32 [1024], P(('dp', 'ctx')), may hold values from 0 to 63, as said below
Outputs:
- attended: bfloat16 [262144, 128], P(('dp', 'ctx'))
Inputs may be any that keep to these rules, and one draw needn't show every extreme that they name: `dest_group`: each device sends its 8 blocks to 8 different sequences, and every device receives exactly 8 blocks, each from a different device along dp with the same ctx index. `block_pos`: in each sequence every block position occurs once; a block that arrives at ctx index c holds a position from c * 8 to c * 8 + 7.
All inputs are finite; a program needn't handle non-finite values.
Results may differ from a plain program's by a relative error of at most 0.0065.
Values may be sent and summed in bfloat16 or wider, within the bound.
A program may use at most 64 MiB of HBM per device.

v0:
```python
import math

import jax
import jax.numpy as jnp
from jax import lax
from jax.sharding import PartitionSpec as P

masked_score = -1e30


def as_sent(x):

    def short(part):
        return part.astype(jnp.bfloat16) if part.dtype == jnp.float32 else part

    return jax.tree.map(short, x)


def document_of(positions, doc_starts):
    return jnp.sum((positions[:, None] >= doc_starts[None, :]).astype(jnp.int32), axis=1)


def tile_update(
    carried, query_tile, query_pos, query_doc, key_tile, value_tile, key_pos, key_doc, score_scale
):
    row_peak, weight_sum, accumulated = carried
    scores = (
        jnp.einsum("qh,kh->qk", query_tile, key_tile, preferred_element_type=jnp.float32)
        * score_scale
    )
    allowed = (key_doc[None, :] == query_doc[:, None]) & (key_pos[None, :] <= query_pos[:, None])
    scores = jnp.where(allowed, scores, masked_score)
    new_peak = jnp.maximum(row_peak, jnp.max(scores, axis=1))
    weights = jnp.where(allowed, jnp.exp(scores - new_peak[:, None]), 0.0)
    factor = jnp.exp(row_peak - new_peak)
    weight_sum = weight_sum * factor + jnp.sum(weights, axis=1)
    accumulated = accumulated * factor[:, None] + jnp.dot(
        weights.astype(jnp.bfloat16), value_tile, preferred_element_type=jnp.float32
    )
    return (new_peak, weight_sum, accumulated)


def make_fold(my_query, my_pos, my_doc, doc_starts, tile_width):
    row_count, head_size = my_query.shape
    query_width = min(row_count, 512)
    block_count = row_count // query_width
    score_scale = 1.0 / math.sqrt(head_size)
    query_blocks = my_query.reshape(block_count, query_width, head_size)
    pos_blocks = my_pos.reshape(block_count, query_width)
    doc_blocks = my_doc.reshape(block_count, query_width)

    def fold_keys(carried, gathered_piece, start_row):
        key_piece, value_piece, key_positions = gathered_piece
        key_docs = document_of(key_positions, doc_starts)
        key_count = key_piece.shape[0]
        key_width = min(key_count, tile_width)
        tile_count = key_count // key_width
        key_tiles = (
            key_piece.reshape(tile_count, key_width, head_size),
            value_piece.reshape(tile_count, key_width, head_size),
            key_positions.reshape(tile_count, key_width),
            key_docs.reshape(tile_count, key_width),
        )

        def per_block(unused, operands):
            query_tile, query_pos, query_doc, row_peak, weight_sum, accumulated = operands

            def per_tile(current, one_tile):
                key_tile, value_tile, tile_pos, tile_doc = one_tile
                updated = tile_update(
                    current,
                    query_tile,
                    query_pos,
                    query_doc,
                    key_tile,
                    value_tile,
                    tile_pos,
                    tile_doc,
                    score_scale,
                )
                return (updated, None)

            finished, unused_out = lax.scan(
                per_tile, (row_peak, weight_sum, accumulated), key_tiles
            )
            return (unused, finished)

        row_peak, weight_sum, accumulated = carried
        unused, results = lax.scan(
            per_block,
            jnp.int32(0),
            (
                query_blocks,
                pos_blocks,
                doc_blocks,
                row_peak.reshape(block_count, query_width),
                weight_sum.reshape(block_count, query_width),
                accumulated.reshape(block_count, query_width, head_size),
            ),
        )
        return (
            results[0].reshape(row_count),
            results[1].reshape(row_count),
            results[2].reshape(row_count, head_size),
        )

    return fold_keys


def shards(query_rows, key_rows, value_rows, doc_lens, dest_group, block_pos):
    group_count = lax.axis_size("dp")
    block_count = dest_group.shape[0]
    row_count, head_size = query_rows.shape
    block_rows = row_count // block_count
    lengths = doc_lens[0]
    doc_starts = jnp.cumsum(lengths) - lengths
    group_ids = jnp.arange(group_count, dtype=jnp.int32)
    matches = dest_group[None, :] == group_ids[:, None]
    source_slot = jnp.sum(
        jnp.where(matches, jnp.arange(block_count, dtype=jnp.int32)[None, :], 0), axis=1
    )
    filled = jnp.any(matches, axis=1)
    stacked = jnp.stack(
        [
            query_rows.reshape(block_count, block_rows, head_size),
            key_rows.reshape(block_count, block_rows, head_size),
            value_rows.reshape(block_count, block_rows, head_size),
        ],
        axis=1,
    )
    outgoing = jnp.where(
        filled[:, None, None, None], stacked[source_slot], jnp.zeros((), stacked.dtype)
    )
    labels = jnp.where(filled, block_pos[source_slot] * block_rows, -1)[:, None]
    arrived, arrived_labels = (
        lax.all_to_all(outgoing, "dp", split_axis=0, concat_axis=0, tiled=True),
        lax.all_to_all(labels, "dp", split_axis=0, concat_axis=0, tiled=True),
    )
    starts_in = arrived_labels[:, 0]
    is_live = starts_in >= 0
    earlier = is_live[None, :] & (starts_in[None, :] < starts_in[:, None])
    order_rank = jnp.sum(earlier.astype(jnp.int32), axis=1)
    unit_count = row_count // block_rows
    wanted = jnp.arange(unit_count, dtype=jnp.int32)
    slot_ids = jnp.arange(starts_in.shape[0], dtype=jnp.int32)
    picked = is_live[None, :] & (order_rank[None, :] == wanted[:, None])
    chosen = jnp.sum(jnp.where(picked, slot_ids[None, :], 0), axis=1)
    my_units = arrived[chosen]
    my_query = my_units[:, 0].reshape(row_count, head_size)
    my_key = my_units[:, 1].reshape(row_count, head_size)
    my_value = my_units[:, 2].reshape(row_count, head_size)
    my_pos = (
        starts_in[chosen][:, None] + jnp.arange(block_rows, dtype=jnp.int32)[None, :]
    ).reshape(row_count)
    my_doc = document_of(my_pos, doc_starts)
    tile_width = 2048
    fold_keys = make_fold(my_query, my_pos, my_doc, doc_starts, tile_width)
    initial = (
        jnp.full((row_count,), masked_score, jnp.float32),
        jnp.zeros((row_count,), jnp.float32),
        jnp.zeros((row_count, head_size), jnp.float32),
    )
    row_peak, weight_sum, accumulated = fold_keys(
        initial,
        (
            lax.all_gather(my_key, "ctx", axis=0, tiled=True),
            lax.all_gather(my_value, "ctx", axis=0, tiled=True),
            lax.all_gather(as_sent(my_pos), "ctx", axis=0, tiled=True),
        ),
        jnp.int32(0),
    )
    attended = (
        (accumulated / weight_sum[:, None])
        .astype(jnp.bfloat16)
        .reshape(unit_count, block_rows, head_size)
    )
    outbound = jnp.where(
        is_live[:, None, None],
        attended[jnp.clip(order_rank, 0, unit_count - 1)],
        jnp.zeros((), jnp.bfloat16),
    )
    returned = lax.all_to_all(outbound, "dp", split_axis=0, concat_axis=0, tiled=True)
    return returned[dest_group].reshape(row_count, head_size)


def solution(mesh):
    return jax.shard_map(
        shards,
        mesh=mesh,
        in_specs=(
            P(("dp", "ctx"), None),
            P(("dp", "ctx"), None),
            P(("dp", "ctx"), None),
            P("dp", None),
            P(("dp", "ctx")),
            P(("dp", "ctx")),
        ),
        out_specs=P(("dp", "ctx"), None),
        check_vma=False,
    )
```

profile of v0, /device:TPU:25, one launch (start us, length us, event | category | flops | bytes accessed | tf_op | source)
XLA Modules:
  0.0 586.8 jit_solution(10386720644248712875)
XLA Ops:
  9.4 6.3 %all-to-all-start = ((s32[16,1,1]{2,1,0:T(1,128)}), s32[16,1,1]{2,1,0:T(1,128)S(1)}, u32[]{:S(2)}, u32[]{:S(2)}) async-start(s32[16,1,1]{2,1,0:T(1,128)} %copy.9), calls=%async_computation | async-start | bytes 16384 | tf_op jit(solution)/shard_map/all_to_all | solution.py:137
  19.9 3.8 broadcast_select_fusion
  23.7 5.7 all-to-all-start.1
  30.2 41.2 %all-to-all-done.1 = bf16[16,3,256,128]{3,2,1,0:T(8,128)(2,1)S(1)} async-done(((bf16[16,3,256,128]{3,2,1,0:T(8,128)(2,1)}), bf16[16,3,256,128]{3,2,1,0:T(8,128)(2,1)S(1)}, u32[]{:S(2)}, u32[]{:S(2)}) %all-to-all-start.1) | async-done | bytes 3145760 | tf_op jit(solution)/shard_map/all_to_all | solution.py:136
  77.7 27.9 %all_gather.9 = s32[16384]{0:T(1024)S(1)} all-gather(s32[2048]{0:T(1024)S(1)} %bitcast.108), channel_id=1, replica_groups=mesh['dp'=16,'ctx'=8] {'ctx'}, dimensions={0}, use_global_device_ids=true | all-gather | bytes 73728 | tf_op jit(solution)/shard_map/all_gather | solution.py:168
  107.7 38.8 %all-gather.3.cloned.1.call-done = bf16[16384,128]{1,0:T(8,128)(2,1)} async-done(((bf16[2048,128]{1,0:T(8,128)(2,1)}), bf16[16384,128]{1,0:T(8,128)(2,1)}) %all-gather.3.cloned.1.call-update) | async-done | bytes 4194320 | tf_op jit(solution)/shard_map/all_gather | solution.py:166
  146.5 71.7 %all-gather.5.cloned.1.call-done = bf16[16384,128]{1,0:T(8,128)(2,1)} async-done(((bf16[2048,128]{1,0:T(8,128)(2,1)}), bf16[16384,128]{1,0:T(8,128)(2,1)}) %all-gather.5.cloned.1.call-update) | async-done | bytes 4194320 | tf_op jit(solution)/shard_map/all_gather | solution.py:167
  218.1 336.7 %while.28 = (s32[]{:T(128)}, f32[4,512]{1,0:T(4,128)S(1)}, f32[4,512,128]{2,1,0:T(8,128)S(1)}, bf16[4,512,128]{2,1,0:T(8,128)(2,1)S(1)}, s32[4,512]{1,0:T(4,128)...) while((s32[]{:T(128)}, f32[4,512]{1,0:T(4,128)S(1)}, ...), condition=%wide.region_12.13_spmd, body=%wide.region_7.12_spmd.sunk | while | flops 560138752 | bytes 31991212 | solution.py:89
  218.2 84.0 %while.29 = (s32[]{:T(128)}, f32[512]{0:T(512)S(1)}, f32[512]{0:T(512)S(1)}, f32[512,128]{1,0:T(8,128)S(1)}, s32[8,2048]{1,0:T(8,128)S(1)}, /*index=5*/s32[512]{...) while((s32[]{:T(128)}, f32[512]{0:T(512)S(1)}, ...), condition=%wide.region_11.11_spmd.clone, body=%wide.region_8.10_spmd.clone.sunk | while | flops 560138752 | bytes 31192232 | solution.py:83
  221.7 4.0 fusion.37
  232.2 4.0 fusion.37
  242.7 4.0 fusion.37
  253.2 4.0 fusion.37
  263.7 4.0 fusion.37
  274.2 4.0 fusion.37
  284.7 4.0 fusion.37
  295.2 4.0 fusion.37
  302.4 84.0 %while.29 = (s32[]{:T(128)}, f32[512]{0:T(512)S(1)}, f32[512]{0:T(512)S(1)}, f32[512,128]{1,0:T(8,128)S(1)}, s32[8,2048]{1,0:T(8,128)S(1)}, /*index=5*/s32[512]{...) while((s32[]{:T(128)}, f32[512]{0:T(512)S(1)}, ...), condition=%wide.region_11.11_spmd.clone, body=%wide.region_8.10_spmd.clone.sunk | while | flops 560138752 | bytes 31192232 | solution.py:83
  305.9 4.0 fusion.37
  316.4 4.0 fusion.37
  326.9 4.0 fusion.37
  337.4 4.0 fusion.37
  347.9 4.0 fusion.37
  358.4 4.0 fusion.37
  368.9 4.0 fusion.37
  379.4 4.0 fusion.37
  386.6 84.0 %while.29 = (s32[]{:T(128)}, f32[512]{0:T(512)S(1)}, f32[512]{0:T(512)S(1)}, f32[512,128]{1,0:T(8,128)S(1)}, s32[8,2048]{1,0:T(8,128)S(1)}, /*index=5*/s32[512]{...) while((s32[]{:T(128)}, f32[512]{0:T(512)S(1)}, ...), condition=%wide.region_11.11_spmd.clone, body=%wide.region_8.10_spmd.clone.sunk | while | flops 560138752 | bytes 31192232 | solution.py:83
  390.1 4.0 fusion.37
  400.6 4.0 fusion.37
  411.1 4.0 fusion.37
  421.6 4.0 fusion.37
  432.1 4.0 fusion.37
  442.6 4.0 fusion.37
  453.1 4.0 fusion.37
  463.6 4.0 fusion.37
  470.8 84.0 %while.29 = (s32[]{:T(128)}, f32[512]{0:T(512)S(1)}, f32[512]{0:T(512)S(1)}, f32[512,128]{1,0:T(8,128)S(1)}, s32[8,2048]{1,0:T(8,128)S(1)}, /*index=5*/s32[512]{...) while((s32[]{:T(128)}, f32[512]{0:T(512)S(1)}, ...), condition=%wide.region_11.11_spmd.clone, body=%wide.region_8.10_spmd.clone.sunk | while | flops 560138752 | bytes 31192232 | solution.py:83
  474.3 4.0 fusion.37
  484.8 4.0 fusion.37
  491.8 3.5 fusion.36
  495.3 4.0 fusion.37
  505.8 4.0 fusion.37
  516.3 4.0 fusion.37
  523.3 3.5 fusion.36
  526.8 4.0 fusion.37
  537.3 4.0 fusion.37
  547.8 4.0 fusion.37
  557.3 5.4 all-to-all-start.2
  562.7 15.8 %all-to-all-done.2 = bf16[16,256,128]{2,1,0:T(8,128)(2,1)S(1)} async-done(((bf16[16,256,128]{2,1,0:T(8,128)(2,1)}), bf16[16,256,128]{2,1,0:T(8,128)(2,1)S(1)}, u32[]{:S(2)}, u32[]{:S(2)}) %all-to-all-start.2) | async-done | bytes 1048608 | tf_op jit(solution)/shard_map/all_to_all | solution.py:182
  (340 shorter events, 220.5 us)
Async XLA Ops:
  6.5 1.5 copy-start
  9.4 14.3 %all-to-all-start = ((s32[16,1,1]{2,1,0:T(1,128)}), s32[16,1,1]{2,1,0:T(1,128)S(1)}, u32[]{:S(2)}, u32[]{:S(2)}) async-start(s32[16,1,1]{2,1,0:T(1,128)} %copy.9), calls=%async_computation | async-start | bytes 16384 | tf_op jit(solution)/shard_map/all_to_all | solution.py:137
  23.7 47.7 %all-to-all-start.1 = ((bf16[16,3,256,128]{3,2,1,0:T(8,128)(2,1)}), bf16[16,3,256,128]{3,2,1,0:T(8,128)(2,1)S(1)}, u32[]{:S(2)}, u32[]{:S(2)}) async-start(bf16[16,3,256,128]{3,2,1,0:T(8,128)(2,1)} %broadcast_select_fusion), calls=%async_computation.1 | async-start | bytes 6291456 | tf_op jit(solution)/shard_map/all_to_all | solution.py:136
  29.5 47.2 %copy-start.3 = (s32[1,4]{1,0:T(1,128)S(1)}, s32[1,4]{1,0:T(1,128)}, u32[]{:S(2)}) copy-start(s32[1,4]{1,0:T(1,128)} %param.13) | copy-start | bytes 52
  29.5 117.0 %all-gather.3.cloned.1.call-start = ((), (), s32[]{:S(2)}) async-start(), calls=%async_computation.3 | async-start | bytes 4718592 | tf_op jit(solution)/shard_map/all_gather | solution.py:166
  75.9 142.2 %all-gather.5.cloned.1.call-start = ((), (), s32[]{:S(2)}) async-start(), calls=%async_computation.4 | async-start | bytes 4718592 | tf_op jit(solution)/shard_map/all_gather | solution.py:167
  218.1 338.0 %copy-start.2 = (pred[16]{0:T(512)(128)(4,1)S(1)}, pred[16]{0:T(512)(128)(4,1)}, u32[]{:S(2)}) copy-start(pred[16]{0:T(512)(128)(4,1)} %compare_reduce_fusion) | copy-start | bytes 52
  221.7 4.0 copy-start.1
  232.2 4.0 copy-start.1
  242.7 4.0 copy-start.1
  253.2 4.0 copy-start.1
  263.7 4.0 copy-start.1
  274.2 4.0 copy-start.1
  284.7 4.0 copy-start.1
  295.2 4.0 copy-start.1
  305.9 4.0 copy-start.1
  316.4 4.0 copy-start.1
  326.9 4.0 copy-start.1
  337.4 4.0 copy-start.1
  347.9 4.0 copy-start.1
  358.4 4.0 copy-start.1
  368.9 4.0 copy-start.1
  379.4 4.0 copy-start.1
  390.1 4.0 copy-start.1
  400.6 4.0 copy-start.1
  411.1 4.0 copy-start.1
  421.6 4.0 copy-start.1
  432.1 4.0 copy-start.1
  442.6 4.0 copy-start.1
  453.1 4.0 copy-start.1
  463.6 4.0 copy-start.1
  474.3 4.0 copy-start.1
  484.8 4.0 copy-start.1
  495.3 4.0 copy-start.1
  505.8 4.0 copy-start.1
  516.3 4.0 copy-start.1
  526.8 4.0 copy-start.1
  537.3 4.0 copy-start.1
  547.8 4.0 copy-start.1
  554.9 7.8 %copy-start.4 = (s32[8]{0:T(128)S(1)}, s32[8]{0:T(128)}, u32[]{:S(2)}) copy-start(s32[8]{0:T(128)} %param.14) | copy-start | bytes 100
  557.3 21.3 %all-to-all-start.2 = ((bf16[16,256,128]{2,1,0:T(8,128)(2,1)}), bf16[16,256,128]{2,1,0:T(8,128)(2,1)S(1)}, u32[]{:S(2)}, u32[]{:S(2)}) async-start(bf16[16,256,128]{2,1,0:T(8,128)(2,1)} %broadcast_select_fusion.1), calls=%async_computation.2 | async-start | bytes 2097152 | tf_op jit(solution)/shard_map/all_to_all | solution.py:182
Sparse Core Ops, SparseCore 0:
  76.0 70.4 all-gather.2
  148.8 69.2 all-gather.4
where the time goes:
time: 593 us; the launch traced here: 587 us
  matrix products  206 us (35%)
  waiting for transfers between devices  168 us (28%)
  other arithmetic  139 us (23%)
  blocking collectives  27.9 us (5%)
  starting transfers between devices  17.6 us (3%)
  between operations  13.6 us (2%)
  local copies, waits for them, and re-layouts  12.7 us (2%)
    reduce_sum x32, other arithmetic, tile_update(): weight_sum = weight_sum * factor + jnp.sum(weights, axis=1)  127 us
    dot_general x32, matrix products, tile_update(): jnp.einsum('qh,kh->qk', query_tile, key_tile, preferred_element_type=jnp....  111 us
    dot_general x32, matrix products, tile_update(): jnp.dot(weights.astype(jnp.bfloat16), value_tile, preferred_element_type=...  94.6 us
    all_gather x1, waiting for transfers between devices, shards(): lax.all_gather(my_value, 'ctx', axis=0, tiled=True)  71.7 us
    all_to_all x1, waiting for transfers between devices, shards(): lax.all_to_all(outgoing, 'dp', split_axis=0, concat_axis=0, tiled=True)  41.2 us
    all_gather x1, waiting for transfers between devices, shards(): lax.all_gather(my_key, 'ctx', axis=0, tiled=True)  38.8 us
    all_gather x1, blocking collectives, shards(): lax.all_gather(as_sent(my_pos), 'ctx', axis=0, tiled=True)  27.9 us
    all_to_all x1, waiting for transfers between devices, shards(): lax.all_to_all(outbound, 'dp', split_axis=0, concat_axis=0, tiled=True)  15.8 us
  transfers between devices with their start and end apart: 5, of which 4 were waited for; matrix products, arithmetic and copies ran while one was open for 2% of the time, Pallas kernels for 0%

commit v1 on v0

v1 whole, which is shorter than its diff:
```python
import functools
import math

import jax
import jax.numpy as jnp
from jax import lax
from jax.experimental import pallas as pl
from jax.experimental.pallas import tpu as pltpu
from jax.sharding import PartitionSpec as P

HEAD = 128
BLK = 256
NB = 8
HALF = BLK // 2
RING = 4
GROUPS = 16
PARTS = 2
SEG = NB * BLK
UNIT = NB * HALF
EXP_SCALE = math.log2(math.e) / math.sqrt(HEAD)
FAR = -(2.0**40)
EMPTY = -1e30
MESH = pl.DeviceIdType.MESH
NT = (((1,), (1,)), ((), ()))


def widened(left, right):
    return jnp.concatenate([left, right], axis=1)


def attend_tiles(tiles, query_of, key_of, value_of, mask_of, peak_ref, acc_ref):
    def scores_of(tile):
        rows, keys = tile
        found = lax.dot_general(
            query_of(rows), key_of(keys), NT, preferred_element_type=jnp.float32
        )
        return found if mask_of is None else jnp.where(mask_of(rows, keys), found, FAR)

    scores = scores_of(tiles[0])
    for at, (rows, keys) in enumerate(tiles):
        following = scores_of(tiles[at + 1]) if at + 1 < len(tiles) else None
        old_peak = peak_ref[rows, :]
        peak = jnp.maximum(old_peak, jnp.max(scores, axis=1, keepdims=True))
        factor = jnp.exp2((old_peak - peak) * EXP_SCALE)
        weights = jnp.exp2((scores - peak[:, :1]) * EXP_SCALE).astype(jnp.bfloat16)
        added = jnp.dot(weights, value_of(keys), preferred_element_type=jnp.float32)
        acc_ref[rows, :] = acc_ref[rows, :] * widened(factor, factor) + added
        peak_ref[rows, :] = peak
        scores = following


def kernel(
    q_ref, k_ref, v_ref, len_ref, group_ref, pos_ref, out_ref,
    q_send, q_recv, kv_send, kv_recv_first, kv_recv_second, kv_all, key_doc, query_doc, queries,
    rank_send, rank_recv, krank_recv, rank_smem, krank_smem, doc_own, doc_recv,
    peak, acc, result, back_send, back_recv,
    q_ssem, q_rsem, m_ssem, m_rsem, km_ssem, km_rsem, kv_ssem, kv_rsem,
    ring_ssem, ring_rsem, core_ssem, core_rsem, doc_ssem, doc_rsem,
    back_ssem, back_rsem, local_sem,
):
    dp = lax.axis_index("dp")
    ctx = lax.axis_index("ctx")
    z_lo, x, core = dp // 8, (dp // 2) % 4, dp % 2
    z_hi, y = ctx // RING, ctx % RING
    mirror = 3 - y
    my_seq = z_lo * 8 + x * 2 + z_hi
    own_seg = core * RING + y
    kv_recv = (kv_recv_first, kv_recv_second)
    query_y = y + z_hi * (mirror - y)
    stays = core == z_hi

    def device(z_lo_, x_, core_, z_hi_, y_):
        return (z_lo_ * 8 + x_ * 2 + core_, z_hi_ * RING + y_)

    up = device(z_lo, x, core, z_hi, (y + 1) % RING)
    down = device(z_lo, x, core, z_hi, (y + 3) % RING)
    twin = device(z_lo, x, 1 - core, z_hi, y)

    def remote(src, dst, ssem, rsem, target):
        return pltpu.make_async_remote_copy(
            src_ref=src, dst_ref=dst, send_sem=ssem, recv_sem=rsem,
            device_id=target, device_id_type=MESH,
        )

    def await_bytes(ref, sem):
        pltpu.make_async_copy(ref, ref, sem).wait()

    barrier = pltpu.get_barrier_semaphore()

    def greet(at, unused):
        peer = ((z_lo + at % 2) % 2, (x + (at // 2) % 4) % 4, (core + (at // 8) % 2) % 2, (z_hi + at // 16) % 2)

        @pl.when(at > 0)
        def _():
            pl.semaphore_signal(barrier, inc=1, device_id=device(*peer, y), device_id_type=MESH)

        pl.semaphore_signal(barrier, inc=1, device_id=device(*peer, mirror), device_id_type=MESH)
        return unused

    lax.fori_loop(0, 32, greet, 0)
    for neighbour in (up, down):
        pl.semaphore_signal(barrier, inc=1, device_id=neighbour, device_id_type=MESH)

    lane = lax.broadcasted_iota(jnp.int32, (1, HEAD), 1)
    begin = jnp.zeros((1, HEAD), jnp.int32)
    until = jnp.full((1, HEAD), 1 << 20, jnp.int32)
    total = jnp.int32(0)
    for document in range(4):
        begin = jnp.where(lane == document, total, begin)
        total = total + len_ref[0, document]
        until = jnp.where(lane == document, total, until)
    doc_own[0] = begin
    doc_own[1] = until

    def arrival(seq):
        slot, rank = jnp.int32(0), jnp.int32(-1)
        for block in range(NB):
            hit = group_ref[block] == seq
            slot = jnp.where(hit, block, slot)
            rank = jnp.where(hit, pos_ref[block] % NB, rank)
        return slot, rank

    def target_of(at):
        return (z_lo + at % 2) % 2, (x + at // 4) % 4, (z_hi + (at // 2) % 2) % 2

    def stage(at, unused):
        z_lo_, x_, seq_core = target_of(at)
        slot, rank = arrival(z_lo_ * 8 + x_ * 2 + seq_core)
        rank_send[at] = jnp.full((1, HEAD), rank, jnp.int32)
        block = q_ref[slot]
        q_send[at, 0] = block[:HALF]
        q_send[at, 1] = block[HALF:]
        keys, values = k_ref[slot], v_ref[slot]
        for part in range(PARTS):
            kv_send[part, at, 0] = keys[part * HALF:(part + 1) * HALF]
            kv_send[part, at, 1] = values[part * HALF:(part + 1) * HALF]
        return unused

    lax.fori_loop(0, GROUPS, stage, 0)
    pl.semaphore_wait(barrier, 65)

    remote(doc_own, doc_recv, doc_ssem, doc_rsem, twin).start()

    def send_ranks(at, unused):
        z_lo_, x_, seq_core = target_of(at)
        for other in range(2):
            half = (core + other) % 2
            here = (at + other == 0) & (query_y == y)

            @pl.when(here)
            def _():
                pltpu.make_async_copy(rank_send.at[at], rank_recv.at[z_hi, dp], m_rsem).start()

            @pl.when(jnp.logical_not(here))
            def _():
                remote(
                    rank_send.at[at], rank_recv.at[z_hi, dp], m_ssem, m_rsem,
                    device(z_lo_, x_, half, seq_core, query_y),
                ).start()

        here = (at == 0) & stays

        @pl.when(here)
        def _():
            pltpu.make_async_copy(rank_send.at[at], krank_recv.at[dp], km_rsem).start()

        @pl.when(jnp.logical_not(here))
        def _():
            remote(
                rank_send.at[at], krank_recv.at[dp], km_ssem, km_rsem, device(z_lo_, x_, z_hi, seq_core, y)
            ).start()

        return unused

    lax.fori_loop(0, GROUPS, send_ranks, 0)

    def send_queries(at, unused):
        z_lo_, x_, seq_core = target_of(at)
        for other in range(2):
            half = (core + other) % 2
            here = (at + other == 0) & (query_y == y)

            @pl.when(here)
            def _():
                pltpu.make_async_copy(q_send.at[at, half], q_recv.at[z_hi, dp], q_rsem).start()

            @pl.when(jnp.logical_not(here))
            def _():
                remote(
                    q_send.at[at, half], q_recv.at[z_hi, dp], q_ssem, q_rsem,
                    device(z_lo_, x_, half, seq_core, query_y),
                ).start()

        return unused

    def send_keys(part):
        def send(at, unused):
            z_lo_, x_, seq_core = target_of(at)
            here = (at == 0) & stays

            @pl.when(here)
            def _():
                pltpu.make_async_copy(kv_send.at[part, at], kv_recv[part].at[dp], kv_rsem.at[part]).start()

            @pl.when(jnp.logical_not(here))
            def _():
                remote(
                    kv_send.at[part, at], kv_recv[part].at[dp], kv_ssem.at[part], kv_rsem.at[part],
                    device(z_lo_, x_, z_hi, seq_core, y),
                ).start()

            return unused

        lax.fori_loop(0, GROUPS, send, 0)

    lax.fori_loop(0, GROUPS, send_queries, 0)
    send_keys(0)
    send_keys(1)

    remote(doc_own, doc_recv, doc_ssem, doc_rsem, twin).wait()
    begin = jnp.where(stays, doc_own[0], doc_recv[0])
    until = jnp.where(stays, doc_own[1], doc_recv[1])
    row = lax.broadcasted_iota(jnp.int32, (HALF, HEAD), 0)
    lanes = lax.broadcasted_iota(jnp.int32, (HALF, HEAD), 1)

    def mark_keys(at, unused):
        part, block = at // (2 * RING * NB), at % (2 * RING * NB)
        place = row + (block * BLK + part * HALF)
        inside = (place >= begin) & (place < until)
        start = pl.multiple_of((block % NB) * HALF, HALF)
        key_doc[part, block // NB, pl.ds(start, HALF), :] = jnp.where(inside, 0.0, FAR).astype(jnp.bfloat16)
        return unused

    lax.fori_loop(0, PARTS * 2 * RING * NB, mark_keys, 0)

    def query_seg(group):
        return y + group * (RING + mirror - y)

    def mark_queries(at, unused):
        group, block = at // NB, at % NB
        place = row + (query_seg(group) * SEG + block * BLK + core * HALF)
        inside = (place >= begin) & (place < until) & (lanes < 4)
        start = pl.multiple_of(block * HALF, HALF)
        query_doc[group, pl.ds(start, HALF), :] = jnp.where(inside, 1.0, 0.0).astype(jnp.bfloat16)
        return unused

    lax.fori_loop(0, 2 * NB, mark_queries, 0)

    def clear(at, unused):
        start = pl.multiple_of(at * HALF, HALF)
        for group in range(2):
            peak[group, pl.ds(start, HALF), :] = jnp.full((HALF, HEAD), EMPTY, jnp.float32)
            acc[group, pl.ds(start, HALF), :] = jnp.zeros((HALF, 2 * HEAD), jnp.float32)
        return unused

    lax.fori_loop(0, NB, clear, 0)

    await_bytes(rank_recv, m_rsem)
    await_bytes(krank_recv, km_rsem)
    ranks_in = pltpu.make_async_copy(rank_recv, rank_smem, local_sem.at[0])
    kranks_in = pltpu.make_async_copy(krank_recv, krank_smem, local_sem.at[1])
    ranks_in.start()
    kranks_in.start()
    ranks_in.wait()
    kranks_in.wait()

    def place_queries(at, unused):
        start = pl.multiple_of(at * HALF, HALF)
        for group in range(2):
            source = jnp.int32(0)
            for sender in range(GROUPS):
                source = jnp.where(rank_smem[group, sender, 0, 0] == at, sender, source)
            queries[group, pl.ds(start, HALF), :] = q_recv[group, source]
        return unused

    def place_keys(part):
        def place(at, unused):
            start = pl.multiple_of(at * HALF, HALF)
            source = jnp.int32(0)
            for sender in range(GROUPS):
                source = jnp.where(krank_smem[sender, 0, 0] == at, sender, source)
            for which in range(2):
                kv_all[part, own_seg, which, pl.ds(start, HALF), :] = kv_recv[part][source, which]
            return unused

        lax.fori_loop(0, NB, place, 0)

    def seg_at(kind, shift):
        return kind * RING + (y + shift) % RING

    def ring_copy(part, which):
        if which == 0:
            here, target = kv_all.at[part, own_seg], up
        elif which == 1:
            here, target = kv_all.at[part, own_seg], down
        elif which == 2:
            here, target = kv_all.at[part, seg_at(core, 3), 0], up
        else:
            here, target = kv_all.at[part, seg_at(core, 1), 1], down
        return remote(here, here, ring_ssem.at[part, which], ring_rsem.at[part, which], target)

    def ring_arrived(part, which):
        if which == 0:
            there = kv_all.at[part, seg_at(core, 3)]
        elif which == 1:
            there = kv_all.at[part, seg_at(core, 1)]
        elif which == 2:
            there = kv_all.at[part, seg_at(core, 2), 0]
        else:
            there = kv_all.at[part, seg_at(core, 2), 1]
        await_bytes(there, ring_rsem.at[part, which])

    shifts = (0, 3, 1, 2)

    def core_copy(part, which):
        here = kv_all.at[part, seg_at(core, shifts[which])]
        return remote(here, here, core_ssem.at[part, which], core_rsem.at[part, which], twin)

    def core_arrived(part, which):
        await_bytes(kv_all.at[part, seg_at(1 - core, shifts[which])], core_rsem.at[part, which])

    def start_part(part):
        await_bytes(kv_recv[part], kv_rsem.at[part])
        place_keys(part)
        ring_copy(part, 0).start()
        ring_copy(part, 1).start()
        core_copy(part, 0).start()

    def next_segment(part, step):
        @pl.when(step == 1)
        def _():
            core_arrived(part, 0)

        @pl.when(step == 2)
        def _():
            ring_arrived(part, 0)
            ring_copy(part, 2).start()
            core_copy(part, 1).start()
            ring_arrived(part, 1)
            ring_copy(part, 3).start()
            core_copy(part, 2).start()

        @pl.when(step == 4)
        def _():
            core_arrived(part, 1)

        @pl.when(step == 5)
        def _():
            core_arrived(part, 2)

        @pl.when(step == 6)
        def _():
            ring_arrived(part, 2)
            ring_arrived(part, 3)
            core_copy(part, 3).start()

        @pl.when(step == 7)
        def _():
            core_arrived(part, 3)

    def unit(part, seg, group, tiles, masked):
        query_row = lax.broadcasted_iota(jnp.int32, (UNIT // 2, 1), 0)

        def mask_of(rows, keys):
            at = query_row + rows.start
            query_place = (at // HALF) * BLK + core * HALF + at % HALF
            key = lax.broadcasted_iota(jnp.int32, (1, keys.size), 1) + keys.start
            key_place = (key // HALF) * BLK + part * HALF + key % HALF
            return key_place <= query_place

        attend_tiles(
            tiles,
            lambda rows: widened(queries[group, rows, :], query_doc[group, rows, :]),
            lambda keys: widened(kv_all[part, seg, 0, keys, :], key_doc[part, seg, keys, :]),
            lambda keys: widened(kv_all[part, seg, 1, keys, :], jnp.ones((keys.size, HEAD), jnp.bfloat16)),
            mask_of if masked else None,
            peak.at[group],
            acc.at[group],
        )

    low, high, whole = pl.ds(0, UNIT // 2), pl.ds(UNIT // 2, UNIT // 2), pl.ds(0, UNIT)

    def visit(at, unused):
        part, step = at // 8, at % 8
        for known in range(PARTS):
            @pl.when(part == known)
            def _():
                next_segment(known, step)

        @pl.when(at == 4)
        def _():
            start_part(1)

        other = jnp.where((step == 1) | (step == 4) | (step == 5) | (step == 7), 1, 0)
        shift = jnp.where((step == 2) | (step == 4), 3, jnp.where((step == 3) | (step == 5), 1, jnp.where(step >= 6, 2, 0)))
        kind = (core + other) % 2
        seg = kind * RING + (y + shift) % RING

        def per_group(group, carried):
            wanted = query_seg(group)

            @pl.when(seg < wanted)
            def _():
                unit(part, seg, group, [(low, whole), (high, whole)], False)

            @pl.when(seg == wanted)
            def _():
                unit(part, seg, group, [(low, low), (high, whole)], True)

            return carried

        return lax.fori_loop(0, 2, per_group, unused)

    await_bytes(q_recv, q_rsem)
    lax.fori_loop(0, NB, place_queries, 0)
    start_part(0)
    lax.fori_loop(0, 8 * PARTS, visit, 0)

    def finish(at, unused):
        start = pl.multiple_of(at * HALF, HALF)
        for group in range(2):
            both = acc[group, pl.ds(start, HALF), :]
            result[group, at] = (both[:, :HEAD] / both[:, HEAD:]).astype(jnp.bfloat16)
        return unused

    lax.fori_loop(0, NB, finish, 0)

    def send_back(at, unused):
        z_lo_, x_, core_ = target_of(at)
        core_ = (core + (at // 2) % 2) % 2
        sender = z_lo_ * 8 + x_ * 2 + core_
        for other in range(2):
            group = (z_hi + other) % 2
            source_y = y + group * (mirror - y)
            rank = jnp.maximum(rank_smem[group, sender, 0, 0], 0)
            back_send[at, other] = result[group, rank]
            here = (at + other == 0) & (source_y == y)

            @pl.when(here)
            def _():
                pltpu.make_async_copy(back_send.at[at, other], back_recv.at[my_seq, core], back_rsem).start()

            @pl.when(jnp.logical_not(here))
            def _():
                remote(
                    back_send.at[at, other], back_recv.at[my_seq, core], back_ssem, back_rsem,
                    device(z_lo_, x_, core_, group, source_y),
                ).start()

        return unused

    lax.fori_loop(0, GROUPS, send_back, 0)
    await_bytes(back_recv, back_rsem)

    def put(at, unused):
        seq = group_ref[at]
        out_ref[at, pl.ds(0, HALF), :] = back_recv[seq, 0]
        out_ref[at, pl.ds(HALF, HALF), :] = back_recv[seq, 1]
        return unused

    lax.fori_loop(0, NB, put, 0)

    sent_all = query_y != y
    back_all = z_hi == 1

    @pl.when(sent_all)
    def _():
        await_bytes(q_send, q_ssem)
        await_bytes(rank_recv, m_ssem)

    @pl.when(jnp.logical_not(sent_all))
    def _():
        await_bytes(q_send.at[pl.ds(0, GROUPS - 1)], q_ssem)
        await_bytes(q_send.at[0, 0], q_ssem)
        await_bytes(rank_recv.at[0], m_ssem)
        await_bytes(rank_recv.at[1, pl.ds(0, GROUPS - 1)], m_ssem)

    @pl.when(back_all)
    def _():
        await_bytes(back_send, back_ssem)

    @pl.when(jnp.logical_not(back_all))
    def _():
        await_bytes(back_send.at[pl.ds(0, GROUPS - 1)], back_ssem)
        await_bytes(back_send.at[0, 0], back_ssem)

    @pl.when(stays)
    def _():
        await_bytes(krank_recv.at[pl.ds(0, GROUPS - 1)], km_ssem)
        for part in range(PARTS):
            await_bytes(kv_send.at[part, pl.ds(0, GROUPS - 1)], kv_ssem.at[part])

    @pl.when(jnp.logical_not(stays))
    def _():
        await_bytes(krank_recv, km_ssem)
        for part in range(PARTS):
            await_bytes(kv_send.at[part], kv_ssem.at[part])

    for part in range(PARTS):
        for which in range(4):
            ring_copy(part, which).wait_send()
            core_copy(part, which).wait_send()


def shards(query_rows, key_rows, value_rows, doc_lens, dest_group, block_pos):
    bf16, i32, f32 = jnp.bfloat16, jnp.int32, jnp.float32
    vmem = pl.BlockSpec(memory_space=pltpu.VMEM)
    smem = pl.BlockSpec(memory_space=pltpu.SMEM)
    dma = pltpu.SemaphoreType.DMA
    blocks = (NB, BLK, HEAD)
    out = pl.pallas_call(
        kernel,
        out_shape=jax.ShapeDtypeStruct(blocks, bf16),
        in_specs=[vmem, vmem, vmem, smem, smem, smem],
        out_specs=vmem,
        scratch_shapes=[
            pltpu.VMEM((GROUPS, 2, HALF, HEAD), bf16),
            pltpu.VMEM((2, GROUPS, HALF, HEAD), bf16),
            pltpu.VMEM((PARTS, GROUPS, 2, HALF, HEAD), bf16),
            pltpu.VMEM((GROUPS, 2, HALF, HEAD), bf16),
            pltpu.VMEM((GROUPS, 2, HALF, HEAD), bf16),
            pltpu.VMEM((PARTS, 2 * RING, 2, UNIT, HEAD), bf16),
            pltpu.VMEM((PARTS, 2 * RING, UNIT, HEAD), bf16),
            pltpu.VMEM((2, UNIT, HEAD), bf16),
            pltpu.VMEM((2, UNIT, HEAD), bf16),
            pltpu.VMEM((GROUPS, 1, HEAD), i32),
            pltpu.VMEM((2, GROUPS, 1, HEAD), i32),
            pltpu.VMEM((GROUPS, 1, HEAD), i32),
            pltpu.SMEM((2, GROUPS, 1, HEAD), i32),
            pltpu.SMEM((GROUPS, 1, HEAD), i32),
            pltpu.VMEM((2, 1, HEAD), i32),
            pltpu.VMEM((2, 1, HEAD), i32),
            pltpu.VMEM((2, UNIT, HEAD), f32),
            pltpu.VMEM((2, UNIT, 2 * HEAD), f32),
            pltpu.VMEM((2, NB, HALF, HEAD), bf16),
            pltpu.VMEM((GROUPS, 2, HALF, HEAD), bf16),
            pltpu.VMEM((GROUPS, 2, HALF, HEAD), bf16),
            dma, dma, dma, dma, dma, dma,
            dma((PARTS,)), dma((PARTS,)),
            dma((PARTS, 4)), dma((PARTS, 4)), dma((PARTS, 4)), dma((PARTS, 4)),
            dma, dma, dma, dma, dma((2,)),
        ],
        compiler_params=pltpu.CompilerParams(
            collective_id=0, has_side_effects=True, vmem_limit_bytes=48 * 2**20
        ),
        name="packed_attention",
    )(
        query_rows.reshape(blocks), key_rows.reshape(blocks), value_rows.reshape(blocks),
        doc_lens, dest_group, block_pos,
    )
    return out.reshape(NB * BLK, HEAD)


def solution(mesh):
    both = P(("dp", "ctx"))
    rows = P(("dp", "ctx"), None)
    return jax.shard_map(
        shards,
        mesh=mesh,
        in_specs=(rows, rows, rows, P("dp", None), both, both),
        out_specs=rows,
        check_vma=False,
    )
```

time: 593 us -> 112 us (0.19)
  matrix products: 206 us -> 0 us
  waiting for transfers between devices: 168 us -> 0 us
  other arithmetic: 139 us -> 0 us
  Pallas kernels: 0 us -> 106 us
  blocking collectives: 27.9 us -> 0 us
  starting transfers between devices: 17.6 us -> 0 us
  between operations: 13.6 us -> 0.02 us
  local copies, waits for them, and re-layouts: 12.7 us -> 4.6 us
    dot_general x64 -> x0, matrix products: 206 us -> none  [the longest x32 111 us: tile_update(): jnp.einsum('qh,kh->qk', query_tile, key_tile, preferred_element_type=jnp....]
    reduce_sum x37 -> x0, other arithmetic: 128 us -> none  [the longest x32 127 us: tile_update(): weight_sum = weight_sum * factor + jnp.sum(weights, axis=1)]
    all_gather x2 -> x0, waiting for transfers between devices: 110 us -> none  [the longest x1 71.7 us: shards(): lax.all_gather(my_value, 'ctx', axis=0, tiled=True)]
    pallas_call x0 -> x1, Pallas kernels: none -> 106 us  [shards(): pl.pallas_call(kernel, out_shape=jax.ShapeDtypeStruct(blocks, bf16), in_s...]
    all_to_all x3 -> x0, waiting for transfers between devices: 57 us -> none  [the longest x1 41.2 us: shards(): lax.all_to_all(outgoing, 'dp', split_axis=0, concat_axis=0, tiled=True)]
    all_gather x1 -> x0, blocking collectives: 27.9 us -> none  [shards(): lax.all_gather(as_sent(my_pos), 'ctx', axis=0, tiled=True)]
    all_to_all x3 -> x0, starting transfers between devices: 17.5 us -> none  [the longest x1 6.34 us: shards(): lax.all_to_all(labels, 'dp', split_axis=0, concat_axis=0, tiled=True)]
    gather x6 -> x0, local copies, waits for them, and re-layouts: 8.09 us -> none  [the longest x1 2.62 us: shards(): stacked[source_slot]]
  transfers between devices with their start and end apart: 5 -> 0, of which waited for: 4 -> 0; matrix products, arithmetic and copies ran while one was open for 2% -> 0% of each run, Pallas kernels for 0% -> 0%
where the time goes in v1:
time: 112 us; the launch traced here: 111 us
  Pallas kernels  106 us (95%)
  local copies, waits for them, and re-layouts  4.6 us (4%)
    pallas_call x1, Pallas kernels, shards(): pl.pallas_call(kernel, out_shape=jax.ShapeDtypeStruct(blocks, bf16), in_s...  106 us
    unnamed x13, local copies, waits for them, and re-layouts  4.6 us

profile of v1, /device:TPU:25, one launch (start us, length us, event | category | flops | bytes accessed | tf_op | source)
XLA Modules:
  0.0 110.6 jit_solution(11006066022749367307)
XLA Ops:
  0.0 0.0 copy-start.3
  0.0 0.0 copy-start.4
  0.0 0.0 copy-start.5
  0.0 0.6 copy-done.3
  0.7 0.0 copy-done.4
  0.7 0.0 copy-done.5
  0.7 0.0 copy-start
  0.7 1.0 copy-done
  1.7 0.0 copy-start.1
  1.7 1.0 copy-done.1
  2.8 0.0 copy-start.2
  2.8 1.0 copy-done.2
  3.8 106.0 %packed_attention.1 = bf16[8,256,128]{2,1,0:T(8,128)(2,1)S(1)} custom-call(bf16[8,256,128]{2,1,0:T(8,128)(2,1)S(1)} %bitcast.5, bf16[8,256,128]{2,1,0:T(8,128)(2,1)S(1)} %bitcast.6, bf16[8,256,128]{2,1,0:T(8,128)(2,1)S(1)} %bitcast.7, s32[1,4]{1,0:T(1,128)S(1)} %copy-done.3, s32[8]{0:T(128)S(1)} %copy-done.4, s32[8]{0:T(128)S(1)} %copy-done.5), custom_call_target="tpu_custom_call" | custom-call | tf_op jit(solution)/shard_map/packed_attention/pallas_call | solution.py:511
  109.8 0.8 copy.8
Async XLA Ops:
  0.0 0.7 copy-start.3
  0.0 0.7 copy-start.4
  0.0 0.7 copy-start.5
  0.7 1.0 copy-start
  1.7 1.0 copy-start.1
  2.8 1.0 copy-start.2

commit v2 on v1

v2 whole, which is shorter than its diff:
```python
import math

import jax
import jax.numpy as jnp
from jax import lax
from jax.experimental import pallas as pl
from jax.experimental.pallas import tpu as pltpu
from jax.sharding import PartitionSpec as P

HEAD = 128
BLK = 256
NB = 8
HALF = BLK // 2
RING = 4
GROUPS = 16
SELF = 6
SEG = NB * BLK
UNIT = NB * HALF
PARTS = 2
PIECE = BLK // PARTS
WIDTH = NB * PIECE
EXP_SCALE = math.log2(math.e) / math.sqrt(HEAD)
FAR = -(2.0**40)
EMPTY = -1e30
MESH = pl.DeviceIdType.MESH
NT = (((1,), (1,)), ((), ()))


def widened(left, right):
    return jnp.concatenate([left, right], axis=1)


def attend_tiles(tiles, query_of, key_of, value_of, mask_of, peak_ref, acc_ref):
    def scores_of(tile):
        rows, keys = tile
        found = lax.dot_general(
            query_of(rows), key_of(keys), NT, preferred_element_type=jnp.float32
        )
        return found if mask_of is None else jnp.where(mask_of(rows, keys), found, FAR)

    scores = scores_of(tiles[0])
    for at, (rows, keys) in enumerate(tiles):
        following = scores_of(tiles[at + 1]) if at + 1 < len(tiles) else None
        old_peak = peak_ref[rows, :]
        peak = jnp.maximum(old_peak, jnp.max(scores, axis=1, keepdims=True))
        factor = jnp.exp2((old_peak - peak) * EXP_SCALE)
        peaks = jnp.concatenate([peak] * (keys.size // HEAD), axis=1)
        weights = jnp.exp2((scores - peaks) * EXP_SCALE).astype(jnp.bfloat16)
        added = jnp.dot(weights, value_of(keys), preferred_element_type=jnp.float32)
        acc_ref[rows, :] = acc_ref[rows, :] * widened(factor, factor) + added
        peak_ref[rows, :] = peak
        scores = following


def kernel(
    q_hbm, k_hbm, v_hbm, len_ref, group_ref, pos_ref, out_ref,
    q_ref, k_ref, v_ref, q_send, q_low, q_high,
    kv_send, kv_recv_0, kv_recv_1, kv_all, key_doc, query_doc, queries,
    rank_send, rank_recv, rank_smem, doc_own, doc_recv,
    peak, acc, result_low, result_high, back_send_low, back_send_high, back_recv,
    in_sem, q_ssem, q_rsem, m_ssem, m_rsem, kv_ssem, kv_rsem,
    ring_ssem, ring_rsem, core_ssem, core_rsem, doc_ssem, doc_rsem,
    back_ssem, back_rsem, local_sem,
):
    dp = lax.axis_index("dp")
    ctx = lax.axis_index("ctx")
    z_lo, x, core = dp // 8, (dp // 2) % 4, dp % 2
    z_hi, y = ctx // RING, ctx % RING
    my_seq = z_lo * 8 + x * 2 + z_hi
    own_seg = core * RING + y
    stays = core == z_hi
    kv_recv = (kv_recv_0, kv_recv_1)
    q_recv = (q_low, q_high)
    result = (result_low, result_high)
    back_send = (back_send_low, back_send_high)

    def device(z_lo_, x_, core_, z_hi_, y_):
        return (z_lo_ * 8 + x_ * 2 + core_, z_hi_ * RING + y_)

    up = device(z_lo, x, core, z_hi, (y + 1) % RING)
    down = device(z_lo, x, core, z_hi, (y + 3) % RING)
    twin = device(z_lo, x, 1 - core, z_hi, y)

    def remote(src, dst, ssem, rsem, target):
        return pltpu.make_async_remote_copy(
            src_ref=src, dst_ref=dst, send_sem=ssem, recv_sem=rsem,
            device_id=target, device_id_type=MESH,
        )

    def await_bytes(ref, sem):
        pltpu.make_async_copy(ref, ref, sem).wait()

    loads = [
        pltpu.make_async_copy(src, dst, in_sem.at[at])
        for at, (src, dst) in enumerate(((q_hbm, q_ref), (k_hbm, k_ref), (v_hbm, v_ref)))
    ]
    for load in loads:
        load.start()

    barrier = pltpu.get_barrier_semaphore()
    for at in range(1, 32):
        peer = device(
            (z_lo + at % 2) % 2, (x + (at // 2) % 4) % 4, (core + (at // 8) % 2) % 2, (z_hi + at // 16) % 2, y
        )
        pl.semaphore_signal(barrier, inc=1, device_id=peer, device_id_type=MESH)
    for neighbour in (up, down):
        pl.semaphore_signal(barrier, inc=1, device_id=neighbour, device_id_type=MESH)

    lane = lax.broadcasted_iota(jnp.int32, (1, HEAD), 1)
    begin = jnp.zeros((1, HEAD), jnp.int32)
    until = jnp.full((1, HEAD), 1 << 20, jnp.int32)
    total = jnp.int32(0)
    for document in range(4):
        begin = jnp.where(lane == document, total, begin)
        total = total + len_ref[0, document]
        until = jnp.where(lane == document, total, until)
    doc_own[0] = begin
    doc_own[1] = until

    def arrival(seq):
        slot, rank = jnp.int32(0), jnp.int32(-1)
        for block in range(NB):
            hit = group_ref[block] == seq
            slot = jnp.where(hit, block, slot)
            rank = jnp.where(hit, pos_ref[block] % NB, rank)
        return slot, rank

    def offsets_of(at):
        z_step = (3 - at // 4 + at % 4) % 4
        return (2 + 3 * (at % 4)) % 4, z_step % 2, z_step // 2

    def target_of(at):
        x_step, z_step, other = offsets_of(at)
        return (z_lo + z_step) % 2, (x + x_step) % 4, (z_hi + other) % 2

    for load in loads:
        load.wait()

    def stage(at, unused):
        z_lo_, x_, seq_core = target_of(at)
        slot, rank = arrival(z_lo_ * 8 + x_ * 2 + seq_core)
        rank_send[at] = jnp.full((1, HEAD), rank, jnp.int32)
        block = q_ref[slot]
        q_send[at, 0] = block[:HALF]
        q_send[at, 1] = block[HALF:]
        keys, values = k_ref[slot], v_ref[slot]
        for part in range(PARTS):
            kv_send[part, at, 0] = keys[part * PIECE:(part + 1) * PIECE]
            kv_send[part, at, 1] = values[part * PIECE:(part + 1) * PIECE]
        return unused

    lax.fori_loop(0, GROUPS, stage, 0)
    pl.semaphore_wait(barrier, 33)

    remote(doc_own, doc_recv, doc_ssem, doc_rsem, twin).start()

    def to_or_here(here, src, dst, ssem, rsem, target):
        @pl.when(here)
        def _():
            pltpu.make_async_copy(src, dst, rsem).start()

        @pl.when(jnp.logical_not(here))
        def _():
            remote(src, dst, ssem, rsem, target).start()

    def send_ranks():
        def send(at, unused):
            z_lo_, x_, seq_core = target_of(at)
            for other in range(2):
                half = (core + other) % 2
                to_or_here(
                    at + other * GROUPS == SELF, rank_send.at[at], rank_recv.at[z_hi, dp], m_ssem, m_rsem,
                    device(z_lo_, x_, half, seq_core, y),
                )
            return unused

        lax.fori_loop(0, GROUPS, send, 0)

    def send_queries(plane):
        def send(at, unused):
            z_lo_, x_, seq_core = target_of(at)
            for other in range(2):
                rows = (core + other) % 2
                to_or_here(
                    at + other * GROUPS == SELF, q_send.at[at, rows], q_recv[plane].at[dp],
                    q_ssem, q_rsem.at[plane], device(z_lo_, x_, rows, seq_core, y),
                )
            return unused

        lax.fori_loop(0, GROUPS, send, 0)

    def queries_sent():
        await_bytes(q_send.at[pl.ds(0, GROUPS - 1)], q_ssem)
        await_bytes(q_send.at[0, 0], q_ssem)

    def send_keys(part):
        def send(at, unused):
            z_lo_, x_, seq_core = target_of(at)
            to_or_here(
                (at == SELF) & stays, kv_send.at[part, at], kv_recv[part].at[dp],
                kv_ssem.at[part], kv_rsem.at[part], device(z_lo_, x_, z_hi, seq_core, y),
            )
            return unused

        lax.fori_loop(0, GROUPS, send, 0)

    def keys_sent(part):
        @pl.when(stays)
        def _():
            await_bytes(kv_send.at[part, pl.ds(0, GROUPS - 1)], kv_ssem.at[part])

        @pl.when(jnp.logical_not(stays))
        def _():
            await_bytes(kv_send.at[part], kv_ssem.at[part])

    def issue(batch):
        @pl.when(z_hi == 0)
        def _():
            send_keys(batch) if batch < PARTS else send_queries(0)

        @pl.when(z_hi == 1)
        def _():
            send_queries(1) if batch == 0 else send_keys(batch - 1)

    def sent(batch):
        @pl.when(z_hi == 0)
        def _():
            keys_sent(batch) if batch < PARTS else queries_sent()

        @pl.when(z_hi == 1)
        def _():
            queries_sent() if batch == 0 else keys_sent(batch - 1)

    send_ranks()
    issue(0)

    remote(doc_own, doc_recv, doc_ssem, doc_rsem, twin).wait()
    begin = jnp.where(stays, doc_own[0], doc_recv[0])
    until = jnp.where(stays, doc_own[1], doc_recv[1])

    def places(first, size):
        return lax.broadcasted_iota(jnp.int32, (size, HEAD), 0) + first

    def key_mark(first, size):
        place = places(first, size)
        return jnp.where((place >= begin) & (place < until), 0.0, FAR).astype(jnp.bfloat16)

    def mark_keys(block, unused):
        rows = pl.ds(pl.multiple_of((block % NB) * PIECE, PIECE), PIECE)
        for part in range(PARTS):
            key_doc[part, block // NB, rows, :] = key_mark(block * BLK + part * PIECE, PIECE)
        return unused

    lax.fori_loop(0, 2 * RING * NB, mark_keys, 0)

    def query_seg(group):
        return y + group * RING

    def prepare(rank, unused):
        rows = pl.ds(pl.multiple_of(rank * HALF, HALF), HALF)
        lanes = lax.broadcasted_iota(jnp.int32, (HALF, HEAD), 1)
        for group in range(2):
            place = places(query_seg(group) * SEG + rank * BLK + core * HALF, HALF)
            inside = (place >= begin) & (place < until) & (lanes < 4)
            query_doc[group, rows, :] = jnp.where(inside, 1.0, 0.0).astype(jnp.bfloat16)
            peak[group, rows, :] = jnp.full((HALF, HEAD), EMPTY, jnp.float32)
            acc[group, rows, :] = jnp.zeros((HALF, 2 * HEAD), jnp.float32)
        return unused

    lax.fori_loop(0, NB, prepare, 0)

    await_bytes(rank_recv, m_rsem)
    ranks_in = pltpu.make_async_copy(rank_recv, rank_smem, local_sem)
    ranks_in.start()
    ranks_in.wait()

    def source_of(plane, rank):
        source = jnp.int32(0)
        for sender in range(GROUPS):
            source = jnp.where(rank_smem[plane, sender, 0, 0] == rank, sender, source)
        return source

    def take_queries(group):
        await_bytes(q_recv[group], q_rsem.at[group])

        def place(rank, unused):
            rows = pl.ds(pl.multiple_of(rank * HALF, HALF), HALF)
            queries[group, rows, :] = q_recv[group][source_of(group, rank)]
            return unused

        lax.fori_loop(0, NB, place, 0)

    def seg_at(kind, shift):
        return kind * RING + (y + shift) % RING

    def kv_at(part, seg):
        return kv_all.at[part, seg]

    def ring_copy(part, which):
        here = (
            kv_at(part, own_seg), kv_at(part, own_seg),
            kv_at(part, seg_at(core, 3)).at[0], kv_at(part, seg_at(core, 1)).at[1],
        )[which]
        return remote(here, here, ring_ssem.at[part, which], ring_rsem.at[part, which], (up, down)[which % 2])

    def ring_arrived(part, which):
        there = (
            kv_at(part, seg_at(core, 3)), kv_at(part, seg_at(core, 1)),
            kv_at(part, seg_at(core, 2)).at[0], kv_at(part, seg_at(core, 2)).at[1],
        )[which]
        await_bytes(there, ring_rsem.at[part, which])

    def shift_of(step):
        return (0, 3, 1, 2)[step]

    def core_copy(part, step):
        here = kv_at(part, seg_at(core, shift_of(step)))
        return remote(here, here, core_ssem.at[part, step], core_rsem.at[part, step], twin)

    def begin_part(part):
        await_bytes(kv_recv[part], kv_rsem.at[part])

        def place(rank, unused):
            rows = pl.ds(pl.multiple_of(rank * PIECE, PIECE), PIECE)
            source = source_of(core, rank)
            for which in range(2):
                kv_all[part, own_seg, which, rows, :] = kv_recv[part][source, which]
            return unused

        lax.fori_loop(0, NB, place, 0)
        ring_copy(part, 0).start()
        ring_copy(part, 1).start()
        core_copy(part, 0).start()

    def pass_on(part):
        ring_arrived(part, 0)
        ring_copy(part, 2).start()
        core_copy(part, 1).start()
        ring_arrived(part, 1)
        ring_copy(part, 3).start()
        core_copy(part, 2).start()

    def complete(part):
        ring_arrived(part, 2)
        ring_arrived(part, 3)
        core_copy(part, 3).start()

    def unit(part, seg, group, tiles, masked):
        def mask_of(rows, keys):
            row = lax.broadcasted_iota(jnp.int32, (rows.size, 1), 0) + rows.start
            key = lax.broadcasted_iota(jnp.int32, (1, keys.size), 1) + keys.start
            query_place = (row // HALF) * BLK + core * HALF + row % HALF
            return (key // PIECE) * BLK + part * PIECE + key % PIECE <= query_place

        attend_tiles(
            tiles,
            lambda rows: widened(queries[group, rows, :], query_doc[group, rows, :]),
            lambda keys: widened(kv_all[part, seg, 0, keys, :], key_doc[part, seg, keys, :]),
            lambda keys: widened(kv_all[part, seg, 1, keys, :], jnp.ones((keys.size, HEAD), jnp.bfloat16)),
            mask_of if masked else None,
            peak.at[group],
            acc.at[group],
        )

    def finish(group):
        def divide(rank, unused):
            both = acc[group, pl.ds(pl.multiple_of(rank * HALF, HALF), HALF), :]
            result[group][rank] = (both[:, :HEAD] / both[:, HEAD:]).astype(jnp.bfloat16)
            return unused

        lax.fori_loop(0, NB, divide, 0)

        def send(at, unused):
            x_step, z_step, other = offsets_of(at)
            z_lo_, x_, core_ = (z_lo + z_step) % 2, (x + x_step) % 4, (core + other) % 2
            rank = jnp.maximum(rank_smem[group, z_lo_ * 8 + x_ * 2 + core_, 0, 0], 0)
            back_send[group][at] = result[group][rank]
            to_or_here(
                (at == SELF) & (z_hi == group), back_send[group].at[at], back_recv.at[my_seq, core],
                back_ssem.at[group], back_rsem, device(z_lo_, x_, core_, group, y),
            )
            return unused

        lax.fori_loop(0, GROUPS, send, 0)

    def visits_of(part, kind, group, fresh, *steps):
        return [(part, kind, step, group, fresh) for step in steps]

    visits = (
        *visits_of(0, 0, 1, 1, 0, 1, 2, 3),
        *visits_of(1, 0, 1, 1, 0),
        *visits_of(0, 1, 1, 1, 0),
        *visits_of(1, 0, 1, 1, 1, 2),
        *visits_of(0, 1, 1, 1, 1, 2),
        *visits_of(0, 0, 0, 0, 0, 1, 2, 3),
        *visits_of(1, 0, 0, 0, 0, 1, 2),
        *visits_of(1, 0, 1, 1, 3),
        *visits_of(0, 1, 1, 1, 3),
        *visits_of(1, 0, 0, 0, 3),
        *visits_of(1, 1, 1, 1, 0, 1, 2, 3),
    )

    def go_on(batch):
        sent(batch - 1)
        issue(batch)

    def on(known, act, part):
        return (known, lambda: act(part))

    actions = {
        1: (on(0, pass_on, 0),),
        3: (on(0, complete, 0),),
        4: (on(None, go_on, 2), on(0, begin_part, 1), on(1, begin_part, 0)),
        6: (on(0, pass_on, 1), on(1, pass_on, 0)),
        8: (on(1, begin_part, 1),),
        10: (on(None, take_queries, 0),),
        12: (on(0, complete, 1), on(1, complete, 0)),
        16: (on(1, pass_on, 1),),
        19: (on(1, complete, 1),),
        20: (on(None, finish, 0),),
    }
    low, high, whole = pl.ds(0, UNIT // 2), pl.ds(UNIT // 2, UNIT // 2), pl.ds(0, WIDTH)
    half = pl.ds(0, WIDTH // 2)

    def pick(at, values):
        found = jnp.int32(values[0])
        for index in range(1, len(values)):
            found = jnp.where(at == index, values[index], found)
        return found

    def visit(at, unused):
        code = pick(at, [(((part * 2 + kind) * RING + step) * 2 + group) * 2 + fresh for part, kind, step, group, fresh in visits])
        part, kind, step, group, fresh = code // 32, (code // 16) % 2, (code // 4) % 4, (code // 2) % 2, code % 2
        for due, listed in actions.items():
            for core_known, act in listed:
                pl.when(at == due if core_known is None else (at == due) & (core == core_known))(act)

        seg = kind * RING + (y + pick(step, (0, 3, 1, 2))) % RING

        @pl.when((fresh == 1) & (kind != core))
        def _():
            await_bytes(kv_all.at[part, seg], core_rsem.at[part, step])

        wanted = query_seg(group)

        @pl.when(seg < wanted)
        def _():
            unit(part, seg, group, [(low, whole), (high, whole)], False)

        @pl.when(seg == wanted)
        def _():
            unit(part, seg, group, [(low, half), (high, whole)], True)

        return unused

    sent(0)
    issue(1)

    @pl.when(core == 0)
    def _():
        begin_part(0)

    take_queries(1)
    lax.fori_loop(0, len(visits), visit, 0)
    finish(1)

    await_bytes(back_recv, back_rsem)

    def put(at, unused):
        seq = group_ref[at]
        out_ref[at, pl.ds(0, HALF), :] = back_recv[seq, 0]
        out_ref[at, pl.ds(HALF, HALF), :] = back_recv[seq, 1]
        return unused

    lax.fori_loop(0, NB, put, 0)

    await_bytes(rank_recv.at[0], m_ssem)
    await_bytes(rank_recv.at[1, pl.ds(0, GROUPS - 1)], m_ssem)
    for group in range(2):
        @pl.when(z_hi == group)
        def _():
            await_bytes(back_send[group].at[pl.ds(0, GROUPS - 1)], back_ssem.at[group])

        @pl.when(z_hi != group)
        def _():
            await_bytes(back_send[group], back_ssem.at[group])

    sent(2)
    for part in range(PARTS):
        for which in range(4):
            ring_copy(part, which).wait_send()
            core_copy(part, which).wait_send()


def shards(query_rows, key_rows, value_rows, doc_lens, dest_group, block_pos):
    bf16, i32, f32 = jnp.bfloat16, jnp.int32, jnp.float32
    vmem = pl.BlockSpec(memory_space=pltpu.VMEM)
    smem = pl.BlockSpec(memory_space=pltpu.SMEM)
    anywhere = pl.BlockSpec(memory_space=pl.ANY)
    dma = pltpu.SemaphoreType.DMA
    blocks = (NB, BLK, HEAD)
    slots = (GROUPS, 2, PIECE, HEAD)
    out = pl.pallas_call(
        kernel,
        out_shape=jax.ShapeDtypeStruct(blocks, bf16),
        in_specs=[anywhere, anywhere, anywhere, smem, smem, smem],
        out_specs=vmem,
        scratch_shapes=[
            pltpu.VMEM(blocks, bf16),
            pltpu.VMEM(blocks, bf16),
            pltpu.VMEM(blocks, bf16),
            pltpu.VMEM((GROUPS, 2, HALF, HEAD), bf16),
            pltpu.VMEM((GROUPS, HALF, HEAD), bf16),
            pltpu.VMEM((GROUPS, HALF, HEAD), bf16),
            pltpu.VMEM((PARTS, *slots), bf16),
            *[pltpu.VMEM(slots, bf16) for _ in range(PARTS)],
            pltpu.VMEM((PARTS, 2 * RING, 2, WIDTH, HEAD), bf16),
            pltpu.VMEM((PARTS, 2 * RING, WIDTH, HEAD), bf16),
            pltpu.VMEM((2, UNIT, HEAD), bf16),
            pltpu.VMEM((2, UNIT, HEAD), bf16),
            pltpu.VMEM((GROUPS, 1, HEAD), i32),
            pltpu.VMEM((2, GROUPS, 1, HEAD), i32),
            pltpu.SMEM((2, GROUPS, 1, HEAD), i32),
            pltpu.VMEM((2, 1, HEAD), i32),
            pltpu.VMEM((2, 1, HEAD), i32),
            pltpu.VMEM((2, UNIT, HEAD), f32),
            pltpu.VMEM((2, UNIT, 2 * HEAD), f32),
            pltpu.VMEM((NB, HALF, HEAD), bf16),
            pltpu.VMEM((NB, HALF, HEAD), bf16),
            pltpu.VMEM((GROUPS, HALF, HEAD), bf16),
            pltpu.VMEM((GROUPS, HALF, HEAD), bf16),
            pltpu.VMEM((GROUPS, 2, HALF, HEAD), bf16),
            dma((3,)), dma, dma((2,)), dma, dma, dma((PARTS,)), dma((PARTS,)),
            dma((PARTS, 4)), dma((PARTS, 4)), dma((PARTS, 4)), dma((PARTS, 4)),
            dma, dma, dma((2,)), dma, dma,
        ],
        compiler_params=pltpu.CompilerParams(
            collective_id=0, has_side_effects=True, vmem_limit_bytes=52 * 2**20
        ),
        name="packed_attention",
    )(
        query_rows.reshape(blocks), key_rows.reshape(blocks), value_rows.reshape(blocks),
        doc_lens, dest_group, block_pos,
    )
    return out.reshape(NB * BLK, HEAD)


def solution(mesh):
    both = P(("dp", "ctx"))
    rows = P(("dp", "ctx"), None)
    return jax.shard_map(
        shards,
        mesh=mesh,
        in_specs=(rows, rows, rows, P("dp", None), both, both),
        out_specs=rows,
        check_vma=False,
    )
```

time: 112 us -> 104 us (0.929)
  Pallas kernels: 106 us -> 99.7 us
    pallas_call x1, Pallas kernels: 106 us -> 99.7 us  [shards(): pl.pallas_call(kernel, out_shape=jax.ShapeDtypeStruct(blocks, bf16), in_s...]
    unnamed x13 -> x11, local copies, waits for them, and re-layouts: 4.6 us -> 3.56 us
where the time goes in v2:
time: 104 us; the launch traced here: 103 us
  Pallas kernels  99.7 us (96%)
  local copies, waits for them, and re-layouts  3.56 us (3%)
    pallas_call x1, Pallas kernels, shards(): pl.pallas_call(kernel, out_shape=jax.ShapeDtypeStruct(blocks, bf16), in_s...  99.7 us
    unnamed x11, local copies, waits for them, and re-layouts  3.56 us

profile of v2, /device:TPU:25, one launch (start us, length us, event | category | flops | bytes accessed | tf_op | source)
XLA Modules:
  0.0 103.3 jit_solution(13042845044481522256)
XLA Ops:
  0.0 0.0 copy-start.2
  0.0 0.0 copy-start.3
  0.0 0.0 copy-start.4
  0.0 0.6 copy-done.2
  0.7 0.0 copy-done.3
  0.7 0.0 copy-done.4
  0.7 0.0 copy-start
  0.7 1.0 %copy-done = bf16[2048,128]{1,0:T(8,128)(2,1)S(1)} copy-done((bf16[2048,128]{1,0:T(8,128)(2,1)S(1)}, bf16[2048,128]{1,0:T(8,128)(2,1)}, u32[]{:S(2)}) %copy-start) | copy-done | bytes 524312
  1.7 0.0 copy-start.1
  1.7 1.0 %copy-done.1 = bf16[2048,128]{1,0:T(8,128)(2,1)S(1)} copy-done((bf16[2048,128]{1,0:T(8,128)(2,1)S(1)}, bf16[2048,128]{1,0:T(8,128)(2,1)}, u32[]{:S(2)}) %copy-start.1) | copy-done | bytes 524312
  2.8 99.7 %packed_attention.1 = bf16[8,256,128]{2,1,0:T(8,128)(2,1)S(1)} custom-call(bf16[8,256,128]{2,1,0:T(8,128)(2,1)S(1)} %bitcast.5, bf16[8,256,128]{2,1,0:T(8,128)(2,1)S(1)} %bitcast.6, bf16[8,256,128]{2,1,0:T(8,128)(2,1)} %bitcast.7, s32[1,4]{1,0:T(1,128)S(1)} %copy-done.2, s32[8]{0:T(128)S(1)} %copy-done.3, s32[8]{0:T(128)S(1)} %copy-done.4), custom_call_target="tpu_custom_call" | custom-call | tf_op jit(solution)/shard_map/packed_attention/pallas_call | solution.py:503
  102.5 0.8 copy.8
Async XLA Ops:
  0.0 0.7 copy-start.2
  0.0 0.7 copy-start.3
  0.0 0.7 copy-start.4
  0.7 1.0 %copy-start = (bf16[2048,128]{1,0:T(8,128)(2,1)S(1)}, bf16[2048,128]{1,0:T(8,128)(2,1)}, u32[]{:S(2)}) copy-start(bf16[2048,128]{1,0:T(8,128)(2,1)} %param.6) | copy-start | bytes 1572868
  1.7 1.0 %copy-start.1 = (bf16[2048,128]{1,0:T(8,128)(2,1)S(1)}, bf16[2048,128]{1,0:T(8,128)(2,1)}, u32[]{:S(2)}) copy-start(bf16[2048,128]{1,0:T(8,128)(2,1)} %param.7) | copy-start | bytes 1572868

commit v3 on v2

--- a/solution.py
+++ b/solution.py
@@ -216,7 +216,7 @@
     def issue(batch):
         @pl.when(z_hi == 0)
         def _():
-            send_keys(batch) if batch < PARTS else send_queries(0)
+            send_queries(0) if batch == 1 else send_keys(batch // 2)
 
         @pl.when(z_hi == 1)
         def _():
@@ -225,7 +225,7 @@
     def sent(batch):
         @pl.when(z_hi == 0)
         def _():
-            keys_sent(batch) if batch < PARTS else queries_sent()
+            queries_sent() if batch == 1 else keys_sent(batch // 2)
 
         @pl.when(z_hi == 1)
         def _():
@@ -388,16 +388,17 @@
 
     visits = (
         *visits_of(0, 0, 1, 1, 0, 1, 2, 3),
+        *visits_of(0, 0, 0, 0, 0, 1, 2, 3),
+        *visits_of(0, 1, 1, 1, 0, 1, 2, 3),
         *visits_of(1, 0, 1, 1, 0),
-        *visits_of(0, 1, 1, 1, 0),
+        *visits_of(1, 0, 0, 0, 0),
+        *visits_of(1, 1, 1, 1, 0),
         *visits_of(1, 0, 1, 1, 1, 2),
-        *visits_of(0, 1, 1, 1, 1, 2),
-        *visits_of(0, 0, 0, 0, 0, 1, 2, 3),
-        *visits_of(1, 0, 0, 0, 0, 1, 2),
+        *visits_of(1, 0, 0, 0, 1, 2),
+        *visits_of(1, 1, 1, 1, 1, 2),
         *visits_of(1, 0, 1, 1, 3),
-        *visits_of(0, 1, 1, 1, 3),
         *visits_of(1, 0, 0, 0, 3),
-        *visits_of(1, 1, 1, 1, 0, 1, 2, 3),
+        *visits_of(1, 1, 1, 1, 3),
     )
 
     def go_on(batch):
@@ -409,15 +410,15 @@
 
     actions = {
         1: (on(0, pass_on, 0),),
+        2: (on(None, go_on, 2), on(1, begin_part, 0)),
         3: (on(0, complete, 0),),
-        4: (on(None, go_on, 2), on(0, begin_part, 1), on(1, begin_part, 0)),
-        6: (on(0, pass_on, 1), on(1, pass_on, 0)),
-        8: (on(1, begin_part, 1),),
-        10: (on(None, take_queries, 0),),
-        12: (on(0, complete, 1), on(1, complete, 0)),
-        16: (on(1, pass_on, 1),),
-        19: (on(1, complete, 1),),
-        20: (on(None, finish, 0),),
+        4: (on(None, take_queries, 0),),
+        7: (on(1, pass_on, 0),),
+        9: (on(None, begin_part, 1),),
+        10: (on(1, complete, 0),),
+        15: (on(None, pass_on, 1),),
+        21: (on(None, complete, 1),),
+        23: (on(None, finish, 0),),
     }
     low, high, whole = pl.ds(0, UNIT // 2), pl.ds(UNIT // 2, UNIT // 2), pl.ds(0, WIDTH)
     half = pl.ds(0, WIDTH // 2)

time: 104 us -> 96.5 us (0.928)
  Pallas kernels: 99.7 us -> 91.5 us
    pallas_call x1, Pallas kernels: 99.7 us -> 91.5 us  [shards(): pl.pallas_call(kernel, out_shape=jax.ShapeDtypeStruct(blocks, bf16), in_s...]
where the time goes in v3:
time: 96.5 us; the launch traced here: 95.1 us
  Pallas kernels  91.5 us (95%)
  local copies, waits for them, and re-layouts  3.56 us (4%)
    pallas_call x1, Pallas kernels, shards(): pl.pallas_call(kernel, out_shape=jax.ShapeDtypeStruct(blocks, bf16), in_s...  91.5 us
    unnamed x11, local copies, waits for them, and re-layouts  3.56 us

profile of v3, /device:TPU:25, one launch (start us, length us, event | category | flops | bytes accessed | tf_op | source)
XLA Modules:
  0.0 95.1 jit_solution(12240219834200114284)
XLA Ops:
  0.0 0.0 copy-start.2
  0.0 0.0 copy-start.3
  0.0 0.0 copy-start.4
  0.0 0.6 copy-done.2
  0.7 0.0 copy-done.3
  0.7 0.0 copy-done.4
  0.7 0.0 copy-start
  0.7 1.0 %copy-done = bf16[2048,128]{1,0:T(8,128)(2,1)S(1)} copy-done((bf16[2048,128]{1,0:T(8,128)(2,1)S(1)}, bf16[2048,128]{1,0:T(8,128)(2,1)}, u32[]{:S(2)}) %copy-start) | copy-done | bytes 524312
  1.7 0.0 copy-start.1
  1.7 1.0 %copy-done.1 = bf16[2048,128]{1,0:T(8,128)(2,1)S(1)} copy-done((bf16[2048,128]{1,0:T(8,128)(2,1)S(1)}, bf16[2048,128]{1,0:T(8,128)(2,1)}, u32[]{:S(2)}) %copy-start.1) | copy-done | bytes 524312
  2.8 91.5 %packed_attention.1 = bf16[8,256,128]{2,1,0:T(8,128)(2,1)S(1)} custom-call(bf16[8,256,128]{2,1,0:T(8,128)(2,1)S(1)} %bitcast.5, bf16[8,256,128]{2,1,0:T(8,128)(2,1)S(1)} %bitcast.6, bf16[8,256,128]{2,1,0:T(8,128)(2,1)} %bitcast.7, s32[1,4]{1,0:T(1,128)S(1)} %copy-done.2, s32[8]{0:T(128)S(1)} %copy-done.3, s32[8]{0:T(128)S(1)} %copy-done.4), custom_call_target="tpu_custom_call" | custom-call | tf_op jit(solution)/shard_map/packed_attention/pallas_call | solution.py:504
  94.3 0.8 copy.8
Async XLA Ops:
  0.0 0.7 copy-start.2
  0.0 0.7 copy-start.3
  0.0 0.7 copy-start.4
  0.7 1.0 %copy-start = (bf16[2048,128]{1,0:T(8,128)(2,1)S(1)}, bf16[2048,128]{1,0:T(8,128)(2,1)}, u32[]{:S(2)}) copy-start(bf16[2048,128]{1,0:T(8,128)(2,1)} %param.6) | copy-start | bytes 1572868
  1.7 1.0 %copy-start.1 = (bf16[2048,128]{1,0:T(8,128)(2,1)S(1)}, bf16[2048,128]{1,0:T(8,128)(2,1)}, u32[]{:S(2)}) copy-start(bf16[2048,128]{1,0:T(8,128)(2,1)} %param.7) | copy-start | bytes 1572868

commit v4 on v3

--- a/solution.py
+++ b/solution.py
@@ -60,7 +60,7 @@
     peak, acc, result_low, result_high, back_send_low, back_send_high, back_recv,
     in_sem, q_ssem, q_rsem, m_ssem, m_rsem, kv_ssem, kv_rsem,
     ring_ssem, ring_rsem, core_ssem, core_rsem, doc_ssem, doc_rsem,
-    back_ssem, back_rsem, local_sem,
+    back_ssem, back_rsem, local_sem, t_ssem, t_rsem,
 ):
     dp = lax.axis_index("dp")
     ctx = lax.axis_index("ctx")
@@ -166,12 +166,10 @@
     def send_ranks():
         def send(at, unused):
             z_lo_, x_, seq_core = target_of(at)
-            for other in range(2):
-                half = (core + other) % 2
-                to_or_here(
-                    at + other * GROUPS == SELF, rank_send.at[at], rank_recv.at[z_hi, dp], m_ssem, m_rsem,
-                    device(z_lo_, x_, half, seq_core, y),
-                )
+            to_or_here(
+                (at == SELF) & stays, rank_send.at[at], rank_recv.at[z_hi, dp], m_ssem, m_rsem,
+                device(z_lo_, x_, z_hi, seq_core, y),
+            )
             return unused
 
         lax.fori_loop(0, GROUPS, send, 0)
@@ -269,7 +267,11 @@
 
     lax.fori_loop(0, NB, prepare, 0)
 
-    await_bytes(rank_recv, m_rsem)
+    await_bytes(rank_recv.at[core], m_rsem)
+    shared = remote(rank_recv.at[core], rank_recv.at[core], t_ssem, t_rsem, twin)
+    shared.start()
+    shared.wait_send()
+    await_bytes(rank_recv.at[1 - core], t_rsem)
     ranks_in = pltpu.make_async_copy(rank_recv, rank_smem, local_sem)
     ranks_in.start()
     ranks_in.wait()
@@ -414,8 +416,7 @@
         3: (on(0, complete, 0),),
         4: (on(None, take_queries, 0),),
         7: (on(1, pass_on, 0),),
-        9: (on(None, begin_part, 1),),
-        10: (on(1, complete, 0),),
+        10: (on(1, complete, 0), on(None, begin_part, 1)),
         15: (on(None, pass_on, 1),),
         21: (on(None, complete, 1),),
         23: (on(None, finish, 0),),
@@ -475,8 +476,14 @@
 
     lax.fori_loop(0, NB, put, 0)
 
-    await_bytes(rank_recv.at[0], m_ssem)
-    await_bytes(rank_recv.at[1, pl.ds(0, GROUPS - 1)], m_ssem)
+    @pl.when(stays)
+    def _():
+        await_bytes(rank_recv.at[0, pl.ds(0, GROUPS - 1)], m_ssem)
+
+    @pl.when(jnp.logical_not(stays))
+    def _():
+        await_bytes(rank_recv.at[0], m_ssem)
+
     for group in range(2):
         @pl.when(z_hi == group)
         def _():
@@ -533,7 +540,7 @@
             pltpu.VMEM((GROUPS, 2, HALF, HEAD), bf16),
             dma((3,)), dma, dma((2,)), dma, dma, dma((PARTS,)), dma((PARTS,)),
             dma((PARTS, 4)), dma((PARTS, 4)), dma((PARTS, 4)), dma((PARTS, 4)),
-            dma, dma, dma((2,)), dma, dma,
+            dma, dma, dma((2,)), dma, dma, dma, dma,
         ],
         compiler_params=pltpu.CompilerParams(
             collective_id=0, has_side_effects=True, vmem_limit_bytes=52 * 2**20

time: 96.5 us -> 95 us (0.984)
  Pallas kernels: 91.5 us -> 90.5 us
    pallas_call x1, Pallas kernels: 91.5 us -> 90.5 us  [shards(): pl.pallas_call(kernel, out_shape=jax.ShapeDtypeStruct(blocks, bf16), in_s...]
where the time goes in v4:
time: 95 us; the launch traced here: 94.1 us
  Pallas kernels  90.5 us (95%)
  local copies, waits for them, and re-layouts  3.56 us (4%)
    pallas_call x1, Pallas kernels, shards(): pl.pallas_call(kernel, out_shape=jax.ShapeDtypeStruct(blocks, bf16), in_s...  90.5 us
    unnamed x11, local copies, waits for them, and re-layouts  3.56 us

profile of v4, /device:TPU:25, one launch (start us, length us, event | category | flops | bytes accessed | tf_op | source)
XLA Modules:
  0.0 94.1 jit_solution(15001622791227593359)
XLA Ops:
  0.0 0.0 copy-start.2
  0.0 0.0 copy-start.3
  0.0 0.0 copy-start.4
  0.0 0.6 copy-done.2
  0.7 0.0 copy-done.3
  0.7 0.0 copy-done.4
  0.7 0.0 copy-start
  0.7 1.0 %copy-done = bf16[2048,128]{1,0:T(8,128)(2,1)S(1)} copy-done((bf16[2048,128]{1,0:T(8,128)(2,1)S(1)}, bf16[2048,128]{1,0:T(8,128)(2,1)}, u32[]{:S(2)}) %copy-start) | copy-done | bytes 524312
  1.7 0.0 copy-start.1
  1.7 1.0 %copy-done.1 = bf16[2048,128]{1,0:T(8,128)(2,1)S(1)} copy-done((bf16[2048,128]{1,0:T(8,128)(2,1)S(1)}, bf16[2048,128]{1,0:T(8,128)(2,1)}, u32[]{:S(2)}) %copy-start.1) | copy-done | bytes 524312
  2.8 90.5 %packed_attention.1 = bf16[8,256,128]{2,1,0:T(8,128)(2,1)S(1)} custom-call(bf16[8,256,128]{2,1,0:T(8,128)(2,1)S(1)} %bitcast.5, bf16[8,256,128]{2,1,0:T(8,128)(2,1)S(1)} %bitcast.6, bf16[8,256,128]{2,1,0:T(8,128)(2,1)} %bitcast.7, s32[1,4]{1,0:T(1,128)S(1)} %copy-done.2, s32[8]{0:T(128)S(1)} %copy-done.3, s32[8]{0:T(128)S(1)} %copy-done.4), custom_call_target="tpu_custom_call" | custom-call | tf_op jit(solution)/shard_map/packed_attention/pallas_call | solution.py:511
  93.3 0.8 copy.8
Async XLA Ops:
  0.0 0.7 copy-start.2
  0.0 0.7 copy-start.3
  0.0 0.7 copy-start.4
  0.7 1.0 %copy-start = (bf16[2048,128]{1,0:T(8,128)(2,1)S(1)}, bf16[2048,128]{1,0:T(8,128)(2,1)}, u32[]{:S(2)}) copy-start(bf16[2048,128]{1,0:T(8,128)(2,1)} %param.6) | copy-start | bytes 1572868
  1.7 1.0 %copy-start.1 = (bf16[2048,128]{1,0:T(8,128)(2,1)S(1)}, bf16[2048,128]{1,0:T(8,128)(2,1)}, u32[]{:S(2)}) copy-start(bf16[2048,128]{1,0:T(8,128)(2,1)} %param.7) | copy-start | bytes 1572868

commit v5 on v4

--- a/solution.py
+++ b/solution.py
@@ -398,8 +398,8 @@
         *visits_of(1, 0, 1, 1, 1, 2),
         *visits_of(1, 0, 0, 0, 1, 2),
         *visits_of(1, 1, 1, 1, 1, 2),
-        *visits_of(1, 0, 1, 1, 3),
-        *visits_of(1, 0, 0, 0, 3),
+        *visits_of(1, 0, 0, 1, 3),
+        *visits_of(1, 0, 1, 0, 3),
         *visits_of(1, 1, 1, 1, 3),
     )
 
@@ -419,7 +419,7 @@
         10: (on(1, complete, 0), on(None, begin_part, 1)),
         15: (on(None, pass_on, 1),),
         21: (on(None, complete, 1),),
-        23: (on(None, finish, 0),),
+        22: (on(None, finish, 0),),
     }
     low, high, whole = pl.ds(0, UNIT // 2), pl.ds(UNIT // 2, UNIT // 2), pl.ds(0, WIDTH)
     half = pl.ds(0, WIDTH // 2)
@@ -451,7 +451,7 @@
 
         @pl.when(seg == wanted)
         def _():
-            unit(part, seg, group, [(low, half), (high, whole)], True)
+            unit(part, seg, group, [(pl.ds(UNIT // 4 * n, UNIT // 4), pl.ds(0, WIDTH // 4 * (n + 1))) for n in range(4)], True)
 
         return unused
 

time: 95 us -> 94.8 us (level)
  no operation moved by 1% of the time
where the time goes in v5:
time: 94.8 us; the launch traced here: 93.8 us
  Pallas kernels  90.3 us (95%)
  local copies, waits for them, and re-layouts  3.56 us (4%)
    pallas_call x1, Pallas kernels, shards(): pl.pallas_call(kernel, out_shape=jax.ShapeDtypeStruct(blocks, bf16), in_s...  90.3 us
    unnamed x11, local copies, waits for them, and re-layouts  3.56 us

profile of v5, /device:TPU:25, one launch (start us, length us, event | category | flops | bytes accessed | tf_op | source)
XLA Modules:
  0.0 93.8 jit_solution(5877739718260389423)
XLA Ops:
  0.0 0.0 copy-start.2
  0.0 0.0 copy-start.3
  0.0 0.0 copy-start.4
  0.0 0.6 copy-done.2
  0.7 0.0 copy-done.3
  0.7 0.0 copy-done.4
  0.7 0.0 copy-start
  0.7 1.0 %copy-done = bf16[2048,128]{1,0:T(8,128)(2,1)S(1)} copy-done((bf16[2048,128]{1,0:T(8,128)(2,1)S(1)}, bf16[2048,128]{1,0:T(8,128)(2,1)}, u32[]{:S(2)}) %copy-start) | copy-done | bytes 524312
  1.7 0.0 copy-start.1
  1.7 1.0 %copy-done.1 = bf16[2048,128]{1,0:T(8,128)(2,1)S(1)} copy-done((bf16[2048,128]{1,0:T(8,128)(2,1)S(1)}, bf16[2048,128]{1,0:T(8,128)(2,1)}, u32[]{:S(2)}) %copy-start.1) | copy-done | bytes 524312
  2.8 90.3 %packed_attention.1 = bf16[8,256,128]{2,1,0:T(8,128)(2,1)S(1)} custom-call(bf16[8,256,128]{2,1,0:T(8,128)(2,1)S(1)} %bitcast.5, bf16[8,256,128]{2,1,0:T(8,128)(2,1)S(1)} %bitcast.6, bf16[8,256,128]{2,1,0:T(8,128)(2,1)} %bitcast.7, s32[1,4]{1,0:T(1,128)S(1)} %copy-done.2, s32[8]{0:T(128)S(1)} %copy-done.3, s32[8]{0:T(128)S(1)} %copy-done.4), custom_call_target="tpu_custom_call" | custom-call | tf_op jit(solution)/shard_map/packed_attention/pallas_call | solution.py:511
  93.0 0.8 copy.8
Async XLA Ops:
  0.0 0.7 copy-start.2
  0.0 0.7 copy-start.3
  0.0 0.7 copy-start.4
  0.7 1.0 %copy-start = (bf16[2048,128]{1,0:T(8,128)(2,1)S(1)}, bf16[2048,128]{1,0:T(8,128)(2,1)}, u32[]{:S(2)}) copy-start(bf16[2048,128]{1,0:T(8,128)(2,1)} %param.6) | copy-start | bytes 1572868
  1.7 1.0 %copy-start.1 = (bf16[2048,128]{1,0:T(8,128)(2,1)S(1)}, bf16[2048,128]{1,0:T(8,128)(2,1)}, u32[]{:S(2)}) copy-start(bf16[2048,128]{1,0:T(8,128)(2,1)} %param.7) | copy-start | bytes 1572868
